TPU v7x, 128 devices: a whole 4x4x4 slice. The times are simulated.
128 devices in a mesh: bin: 8 (over z_hi, y), row: 4 (over x), col: 4 (over z_lo, core).
Axes of the slice: x: 4, y: 4, z: 4 (z_hi: 2, z_lo: 2; z = z_hi * 2 + z_lo), core: 2. Of those that a mesh axis runs over, the one named last changes fastest.
Arguments:
- snapshots: bfloat16 [4096, 64, 64], P('row', 'bin', 'col'), may hold values from -6 to 6
- focus_in: bfloat16 [64, 4096, 128], P('bin', 'row'), may hold values from -0.09375 to 0.09375
- focus_out: bfloat16 [64, 4096, 128], P('bin', 'row'), may hold values from -0.5 to 0.5
- start_basis: float32 [4096, 128], replicated, may hold values from -6 to 6
Outputs:
- covariance: float32 [4096, 4096], P('col', 'row')
- basis_out: float32 [4096, 128], P(('row', 'col'))
All inputs are finite; a program needn't handle non-finite values.
Results may differ from a plain program's by a relative error of at most 0.0045.
Values may be sent and summed in bfloat16 or wider, within the bound.
A program may use at most 128 MiB of HBM per device.

v0:
```python
import math
import jax
import jax.numpy as jnp
from jax import lax
from jax.sharding import PartitionSpec as P

ITERS = 2


def shards(snapshots, focus_in, focus_out, start_basis):
    rows_here, bins_here, snaps_here = snapshots.shape
    bin_count = lax.axis_size("bin")
    row_count = lax.axis_size("row")
    col_count = lax.axis_size("col")
    col_here = lax.axis_index("col")
    row_here = lax.axis_index("row")
    partial_proj = jnp.einsum(
        "mbs,bmr->brs", snapshots, focus_in, preferred_element_type=jnp.float32
    )
    projected = lax.psum(partial_proj, "row").astype(jnp.bfloat16)
    lifted = jnp.einsum("bmr,brs->mbs", focus_out, projected, preferred_element_type=jnp.float32)
    focused = (snapshots.astype(jnp.float32) + lifted).astype(jnp.bfloat16)
    columns = bins_here * snaps_here
    local_rows = focused.reshape(rows_here, columns)
    all_rows = lax.all_gather(local_rows, "row", axis=0, tiled=True)
    array_size = all_rows.shape[0]
    col_block = array_size // col_count
    piece_rows = col_block // bin_count
    scaling = 1.0 / (columns * col_count * bin_count)
    permuted = (
        all_rows.reshape(col_count, bin_count, piece_rows, columns)
        .transpose(1, 0, 2, 3)
        .reshape(array_size, columns)
    )
    share_rows = lax.psum_scatter(
        lax.dot_general(
            permuted, local_rows, (((1,), (1,)), ((), ())), preferred_element_type=jnp.float32
        ),
        ("bin", "col"),
        scatter_dimension=0,
        tiled=True,
    )
    tile_block = lax.all_gather(share_rows, "bin", axis=0, tiled=True)
    covariance = tile_block * scaling
    basis_now = start_basis
    for sweep_index in range(ITERS):
        col_rows = lax.dynamic_slice_in_dim(basis_now, col_here * col_block, col_block, 0)
        partial_image = lax.dot_general(
            covariance,
            col_rows,
            (((0,), (0,)), ((), ())),
            precision=lax.Precision.HIGHEST,
            preferred_element_type=jnp.float32,
        )
        row_sums = lax.psum(partial_image, "col")
        full_image = lax.all_gather(row_sums, "row", axis=0, tiled=True)
        gram_matrix = jnp.dot(
            full_image.T,
            full_image,
            precision=lax.Precision.HIGHEST,
            preferred_element_type=jnp.float32,
        )
        lower_factor = jnp.linalg.cholesky(gram_matrix)
        basis_now = jax.scipy.linalg.solve_triangular(lower_factor, full_image.T, lower=True).T
    out_rows = array_size // (row_count * col_count)
    mine_start = (row_here * col_count + col_here) * out_rows
    basis_out = lax.dynamic_slice_in_dim(basis_now, mine_start, out_rows, 0) * math.sqrt(array_size)
    return (covariance, basis_out)


def solution(mesh):
    in_specs = (P("row", "bin", "col"), P("bin", "row", None), P("bin", "row", None), P())
    out_specs = (P("col", "row"), P(("row", "col"), None))
    return jax.shard_map(shards, mesh=mesh, in_specs=in_specs, out_specs=out_specs, check_vma=False)
```

profile of v0, /device:TPU:1, one launch (start us, length us, event | category | flops | bytes accessed | tf_op | source)
XLA Modules:
  0.0 558.8 jit_solution(16705941478910044841)
XLA Ops:
  7.2 0.0 copy-start
  7.2 0.0 all-gather.5.cloned.1.call-start
  7.2 2.2 fusion.24
  9.4 14.6 %psum.21 = bf16[8,128,16]{1,2,0:T(8,128)(2,1)S(1)} all-reduce(f32[8,128,16]{1,2,0:T(8,128)S(1)} %fusion.24), channel_id=1, replica_groups=mesh['bin'=8,'row'=4,'col'=4] {'row'}, use_global_device_ids=true, to_apply=%region_0.0 | all-reduce | flops 16384 | bytes 98304 | tf_op jit(solution)/shard_map/psum | solution.py:20
  24.1 0.6 fusion.5
  24.7 0.9 copy.12
  25.6 0.0 all-gather.5.cloned.1.call-update
  25.6 0.0 reduce-scatter.2.cloned.1.call-start
  25.6 27.7 %all-gather.5.cloned.1.call-done = bf16[4096,128]{1,0:T(8,128)(2,1)} async-done(((bf16[1024,128]{1,0:T(8,128)(2,1)}), bf16[4096,128]{1,0:T(8,128)(2,1)}) %all-gather.5.cloned.1.call-update) | async-done | bytes 1048592 | tf_op jit(solution)/shard_map/all_gather | solution.py:25
  53.3 1.3 copy.13
  54.7 8.0 %fusion.21 = f32[4096,1024]{1,0:T(8,128)} fusion(bf16[4096,128]{1,0:T(8,128)(2,1)S(1)} %bitcast.49, bf16[1024,128]{0,1:T(8,128)(2,1)S(1)} %bitcast.51), kind=kOutput, calls=%fused_computation.33 | convolution fusion | flops 1073741824 | bytes 18087936 | tf_op jit(solution)/shard_map/dot_general | solution.py:36
  62.7 0.0 reduce-scatter.2.cloned.1.call-update
  62.7 0.0 all-gather.7.cloned.1.call-start
  62.8 184.6 %reduce-scatter.2.cloned.1.call-done = f32[128,1024]{1,0:T(8,128)} async-done(((f32[4096,1024]{1,0:T(8,128)}), f32[128,1024]{1,0:T(8,128)}) %reduce-scatter.2.cloned.1.call-update) | async-done | bytes 524304 | tf_op jit(solution)/shard_map/reduce_scatter | solution.py:35
  247.4 0.0 all-gather.7.cloned.1.call-update
  247.4 0.0 all-reduce.3.cloned.1.call-start
  247.5 77.1 %all-gather.7.cloned.1.call-done = f32[1024,1024]{1,0:T(8,128)} async-done(((f32[128,1024]{1,0:T(8,128)}), f32[1024,1024]{1,0:T(8,128)}) %all-gather.7.cloned.1.call-update) | async-done | bytes 4194320 | tf_op jit(solution)/shard_map/all_gather | solution.py:43
  324.6 2.6 broadcast_multiply_fusion
  327.2 0.0 copy-start.1
  327.2 2.0 copy-done.1
  329.2 8.5 %fusion.8 = f32[1024,128]{1,0:T(8,128)} fusion(f32[1024,1024]{1,0:T(8,128)S(1)} %broadcast_multiply_fusion, f32[4096,128]{1,0:T(8,128)} %param.10, s32[]{:T(128)S(6)} %select_n.10), kind=kOutput, calls=%fused_computation.10 | convolution fusion | flops 1610612736 | bytes 5242884 | tf_op jit(solution)/shard_map/dot_general | solution.py:48
  337.7 0.0 all-reduce.3.cloned.1.call-update
  337.8 0.0 all-gather.9.cloned.1.call-start
  337.8 36.4 %all-reduce.3.cloned.1.call-done = f32[1024,128]{1,0:T(8,128)} async-done(((f32[1024,128]{1,0:T(8,128)}), f32[1024,128]{1,0:T(8,128)}) %all-reduce.3.cloned.1.call-update) | async-done | bytes 524304 | tf_op jit(solution)/shard_map/psum | solution.py:55
  374.3 0.0 all-gather.9.cloned.1.call-update
  374.3 0.2 all-reduce.5.cloned.1.call-start
  374.5 32.6 %all-gather.9.cloned.1.call-done = f32[4096,128]{1,0:T(8,128)} async-done(((f32[1024,128]{1,0:T(8,128)}), f32[4096,128]{1,0:T(8,128)}) %all-gather.9.cloned.1.call-update) | async-done | bytes 2097168 | tf_op jit(solution)/shard_map/all_gather | solution.py:56
  407.1 5.7 %fusion.22 = f32[128,128]{1,0:T(8,128)S(1)} fusion(f32[4096,128]{1,0:T(8,128)} %all-gather.9.cloned.1.call-done), kind=kOutput, calls=%fused_computation.34 | convolution fusion | flops 805306368 | bytes 2162688 | tf_op jit(solution)/shard_map/dot_general | solution.py:57
  412.8 0.1 copy.14
  412.9 11.7 %cholesky.44 = f32[128,128]{1,0:T(8,128)S(1)} custom-call(f32[128,128]{1,0:T(8,128)S(1)} %fusion.15), custom_call_target="Cholesky" | custom-call | tf_op jit(solution)/shard_map/jit(cholesky)/cholesky | solution.py:63
  424.6 0.6 compare_reduce_fusion.1
  425.3 0.7 fusion.10
  425.9 9.8 %custom-call.6 = f32[1,128,128]{1,2,0:T(8,128)S(1)} custom-call(f32[1,128,128]{2,1,0:T(8,128)S(1)} %fusion.10), custom_call_target="InvertDiagBlocksLowerTriangular" | custom-call | tf_op jit(solution)/shard_map/jit(_solve_triangular)/triangular_solve | solution.py:64
  435.8 3.7 fusion.2
  439.4 7.8 %fusion.6 = f32[1024,128]{1,0:T(8,128)} fusion(f32[1024,1024]{1,0:T(8,128)S(1)} %copy-done.2, f32[128,4096]{1,0:T(8,128)S(1)} %fusion.2, s32[]{:T(128)S(6)} %select_n.10), kind=kOutput, calls=%fused_computation.8 | convolution fusion | flops 1610612736 | bytes 5242884 | tf_op jit(solution)/shard_map/dot_general | solution.py:48
  447.2 0.0 all-reduce.5.cloned.1.call-update
  447.3 0.0 all-gather.11.cloned.1.call-start
  447.3 38.3 %all-reduce.5.cloned.1.call-done = f32[1024,128]{1,0:T(8,128)} async-done(((f32[1024,128]{1,0:T(8,128)}), f32[1024,128]{1,0:T(8,128)}) %all-reduce.5.cloned.1.call-update) | async-done | bytes 524304 | tf_op jit(solution)/shard_map/psum | solution.py:55
  485.6 0.0 all-gather.11.cloned.1.call-update
  485.6 33.0 %all-gather.11.cloned.1.call-done = f32[4096,128]{1,0:T(8,128)} async-done(((f32[1024,128]{1,0:T(8,128)}), f32[4096,128]{1,0:T(8,128)}) %all-gather.11.cloned.1.call-update) | async-done | bytes 2097168 | tf_op jit(solution)/shard_map/all_gather | solution.py:56
  518.6 5.7 %fusion.23 = f32[128,128]{1,0:T(8,128)S(1)} fusion(f32[4096,128]{1,0:T(8,128)} %all-gather.11.cloned.1.call-done), kind=kOutput, calls=%fused_computation.35 | convolution fusion | flops 805306368 | bytes 2162688 | tf_op jit(solution)/shard_map/dot_general | solution.py:57
  524.3 0.1 copy.15
  524.4 11.7 %cholesky.55 = f32[128,128]{1,0:T(8,128)S(1)} custom-call(f32[128,128]{1,0:T(8,128)S(1)} %fusion.13), custom_call_target="Cholesky" | custom-call | tf_op jit(solution)/shard_map/jit(cholesky)/cholesky | solution.py:63
  536.1 0.6 compare_reduce_fusion
  536.8 0.7 fusion.11
  537.4 9.8 %custom-call.7 = f32[1,128,128]{1,2,0:T(8,128)S(1)} custom-call(f32[1,128,128]{2,1,0:T(8,128)S(1)} %fusion.11), custom_call_target="InvertDiagBlocksLowerTriangular" | custom-call | tf_op jit(solution)/shard_map/jit(_solve_triangular)/triangular_solve | solution.py:64
  547.3 3.5 fusion
  550.8 0.8 copy.16
  (10 shorter events, 0.1 us)
Async XLA Ops:
  7.2 16.9 %copy-start = (bf16[8,1024,128]{2,1,0:T(8,128)(2,1)S(1)}, bf16[8,1024,128]{2,1,0:T(8,128)(2,1)}, u32[]{:S(2)}) copy-start(bf16[8,1024,128]{2,1,0:T(8,128)(2,1)} %param.9) | copy-start | bytes 6291460
  7.2 16.9 %copy-start.3 = (bf16[1024,8,16]{0,2,1:T(8,128)(2,1)S(1)}, bf16[1024,8,16]{0,2,1:T(8,128)(2,1)}, u32[]{:S(2)}) copy-start(bf16[1024,8,16]{0,2,1:T(8,128)(2,1)} %param.7) | copy-start | bytes 786436
  7.2 46.2 %all-gather.5.cloned.1.call-start = ((), (), s32[]{:S(2)}) async-start(), calls=%async_computation.1 | async-start | bytes 1310720 | tf_op jit(solution)/shard_map/all_gather | solution.py:25
  25.6 221.8 %reduce-scatter.2.cloned.1.call-start = ((), (), s32[]{:S(2)}) async-start(), calls=%async_computation.2 | async-start | bytes 17301504 | tf_op jit(solution)/shard_map/reduce_scatter | solution.py:35
  62.7 261.8 %all-gather.7.cloned.1.call-start = ((), (), s32[]{:S(2)}) async-start(), calls=%async_computation.3 | async-start | bytes 4718592 | tf_op jit(solution)/shard_map/all_gather | solution.py:43
  247.4 126.8 %all-reduce.3.cloned.1.call-start = ((), (), s32[]{:S(2)}) async-start(), calls=%async_computation.4 | async-start | bytes 1048576 | tf_op jit(solution)/shard_map/psum | solution.py:55
  327.2 2.0 copy-start.1
  337.8 69.3 %all-gather.9.cloned.1.call-start = ((), (), s32[]{:S(2)}) async-start(), calls=%async_computation.5 | async-start | bytes 2621440 | tf_op jit(solution)/shard_map/all_gather | solution.py:56
  374.3 111.3 %all-reduce.5.cloned.1.call-start = ((), (), s32[]{:S(2)}) async-start(), calls=%async_computation.6 | async-start | bytes 1048576 | tf_op jit(solution)/shard_map/psum | solution.py:55
  435.7 3.7 copy-start.2
  447.3 71.3 %all-gather.11.cloned.1.call-start = ((), (), s32[]{:S(2)}) async-start(), calls=%async_computation.7 | async-start | bytes 2621440 | tf_op jit(solution)/shard_map/all_gather | solution.py:56
Sparse Core Ops, SparseCore 0:
  25.7 27.5 all-gather.4
  62.9 184.4 reduce-scatter.1
  249.7 74.8 all-gather.6
  337.9 36.3 all-reduce.2
  375.8 31.2 all-gather.8
  447.4 38.1 all-reduce.4
  487.3 31.2 all-gather.10
where the time goes:
time: 567 us; the launch traced here: 559 us
  waiting for transfers between devices  430 us (76%)
  other arithmetic  48.4 us (9%)
  matrix products  45.7 us (8%)
  between operations  14.7 us (3%)
  blocking collectives  14.6 us (3%)
    reduce_scatter x1, waiting for transfers between devices, shards(): lax.psum_scatter(lax.dot_general(permuted, local_rows, (((1,), (1,)), (()...  185 us
    all_gather x1, waiting for transfers between devices, shards(): tile_block = lax.all_gather(share_rows, 'bin', axis=0, tiled=True)  77.1 us
    psum x2, waiting for transfers between devices, shards(): row_sums = lax.psum(partial_image, 'col')  74.7 us
    all_gather x2, waiting for transfers between devices, shards(): full_image = lax.all_gather(row_sums, 'row', axis=0, tiled=True)  65.5 us
    all_gather x1, waiting for transfers between devices, shards(): all_rows = lax.all_gather(local_rows, 'row', axis=0, tiled=True)  27.7 us
    another operation x6, other arithmetic, shards(): lower_factor = jnp.linalg.cholesky(gram_matrix)  24.8 us
    another operation x4, other arithmetic, shards(): jax.scipy.linalg.solve_triangular(lower_factor, full_image.T, lower=True)  20.9 us
    dot_general x2, matrix products, shards(): lax.dot_general(covariance, col_rows, (((0,), (0,)), ((), ())), precision...  16.3 us
  transfers between devices with their start and end apart: 7, of which 7 were waited for; matrix products, arithmetic and copies ran while one was open for 0% of the time, Pallas kernels for 0%

commit v1 on v0

--- a/solution.py
+++ b/solution.py
@@ -53,7 +53,14 @@
             preferred_element_type=jnp.float32,
         )
         row_sums = lax.psum(partial_image, "col")
-        full_image = lax.all_gather(row_sums, "row", axis=0, tiled=True)
+        ring = [row_sums]
+        for hop in range(3):
+            ring.append(lax.ppermute(ring[-1], "row", [(dev, (dev + 1) % 4) for dev in range(4)]))
+        full_image = jnp.roll(
+            jnp.concatenate(ring[::-1], axis=0),
+            (lax.axis_index("row") + 1) * ring[0].shape[0],
+            axis=0,
+        )
         gram_matrix = jnp.dot(
             full_image.T,
             full_image,

time: 567 us -> 595 us (1.049)
  waiting for transfers between devices: 430 us -> 445 us
  other arithmetic: 48.4 us -> 58.6 us
    ppermute x0 -> x6, waiting for transfers between devices: none -> 80.1 us  [shards(): lax.ppermute(ring[-1], 'row', [(dev, (dev + 1) % 4) for dev in range(4)])]
    all_gather x2 -> x0, waiting for transfers between devices: 65.5 us -> none  [shards(): full_image = lax.all_gather(row_sums, 'row', axis=0, tiled=True)]
    concatenate x0 -> x2, other arithmetic: none -> 9.9 us  [shards(): jnp.roll(jnp.concatenate(ring[::-1], axis=0), (lax.axis_index('row') + 1)...]
  transfers between devices with their start and end apart: 7 -> 11, of which waited for: 7 -> 11; matrix products, arithmetic and copies ran while one was open for 0% -> 0% of each run, Pallas kernels for 0% -> 0%
where the time goes in v1:
time: 595 us; the launch traced here: 585 us
  waiting for transfers between devices  445 us (75%)
  other arithmetic  58.6 us (10%)
  matrix products  41.3 us (7%)
  blocking collectives  14.6 us (2%)
  between operations  14.2 us (2%)
  local copies, waits for them, and re-layouts  7.79 us (1%)
    reduce_scatter x1, waiting for transfers between devices, shards(): lax.psum_scatter(lax.dot_general(permuted, local_rows, (((1,), (1,)), (()...  185 us
    ppermute x6, waiting for transfers between devices, shards(): lax.ppermute(ring[-1], 'row', [(dev, (dev + 1) % 4) for dev in range(4)])  80.1 us
    all_gather x1, waiting for transfers between devices, shards(): tile_block = lax.all_gather(share_rows, 'bin', axis=0, tiled=True)  76.4 us
    psum x2, waiting for transfers between devices, shards(): row_sums = lax.psum(partial_image, 'col')  75.5 us
    all_gather x1, waiting for transfers between devices, shards(): all_rows = lax.all_gather(local_rows, 'row', axis=0, tiled=True)  27.7 us
    another operation x6, other arithmetic, shards(): lower_factor = jnp.linalg.cholesky(gram_matrix)  24.8 us
    another operation x4, other arithmetic, shards(): jax.scipy.linalg.solve_triangular(lower_factor, full_image.T, lower=True)  21.3 us
    dot_general x2, matrix products, shards(): lax.dot_general(covariance, col_rows, (((0,), (0,)), ((), ())), precision...  16.1 us
  transfers between devices with their start and end apart: 11, of which 11 were waited for; matrix products, arithmetic and copies ran while one was open for 0% of the time, Pallas kernels for 0%

profile of v1, /device:TPU:1, one launch (start us, length us, event | category | flops | bytes accessed | tf_op | source)
XLA Modules:
  0.0 584.8 jit_solution(3483945770121792039)
XLA Ops:
  7.2 2.2 fusion.38
  9.4 14.6 %psum.21 = bf16[8,128,16]{1,2,0:T(8,128)(2,1)S(1)} all-reduce(f32[8,128,16]{1,2,0:T(8,128)S(1)} %fusion.38), channel_id=1, replica_groups=mesh['bin'=8,'row'=4,'col'=4] {'row'}, use_global_device_ids=true, to_apply=%region_0.0 | all-reduce | flops 16384 | bytes 98304 | tf_op jit(solution)/shard_map/psum | solution.py:20
  24.1 0.6 fusion.19
  24.7 0.9 copy.12
  25.6 0.0 reduce-scatter.2.cloned.1.call-start
  25.6 27.7 %all-gather.3.cloned.1.call-done = bf16[4096,128]{1,0:T(8,128)(2,1)} async-done(((bf16[1024,128]{1,0:T(8,128)(2,1)}), bf16[4096,128]{1,0:T(8,128)(2,1)}) %all-gather.3.cloned.1.call-update) | async-done | bytes 1048592 | tf_op jit(solution)/shard_map/all_gather | solution.py:25
  53.3 1.3 copy.13
  54.7 8.1 %fusion.35 = f32[4096,1024]{1,0:T(8,128)} fusion(bf16[4096,128]{1,0:T(8,128)(2,1)S(1)} %bitcast.49, bf16[1024,128]{0,1:T(8,128)(2,1)S(1)} %bitcast.51), kind=kOutput, calls=%fused_computation.63 | convolution fusion | flops 1073741824 | bytes 18087936 | tf_op jit(solution)/shard_map/dot_general | solution.py:36
  62.8 0.0 all-gather.5.cloned.1.call-start
  62.8 185.3 %reduce-scatter.2.cloned.1.call-done = f32[128,1024]{1,0:T(8,128)} async-done(((f32[4096,1024]{1,0:T(8,128)}), f32[128,1024]{1,0:T(8,128)}) %reduce-scatter.2.cloned.1.call-update) | async-done | bytes 524304 | tf_op jit(solution)/shard_map/reduce_scatter | solution.py:35
  248.1 0.0 all-reduce.3.cloned.1.call-start
  248.2 76.4 %all-gather.5.cloned.1.call-done = f32[1024,1024]{1,0:T(8,128)} async-done(((f32[128,1024]{1,0:T(8,128)}), f32[1024,1024]{1,0:T(8,128)}) %all-gather.5.cloned.1.call-update) | async-done | bytes 4194320 | tf_op jit(solution)/shard_map/all_gather | solution.py:43
  324.6 2.6 broadcast_multiply_fusion
  327.3 2.0 copy-done.1
  329.3 8.5 %fusion.22 = f32[1024,128]{1,0:T(8,128)} fusion(f32[1024,1024]{1,0:T(8,128)S(1)} %broadcast_multiply_fusion, f32[4096,128]{1,0:T(8,128)} %param.12, s32[]{:T(128)S(6)} %select_n.20), kind=kOutput, calls=%fused_computation.40 | convolution fusion | flops 1610612736 | bytes 5242884 | tf_op jit(solution)/shard_map/dot_general | solution.py:48
  337.8 0.0 all-reduce.5.cloned.1.call-start
  337.8 36.4 %all-reduce.3.cloned.1.call-done = f32[1024,128]{1,0:T(8,128)} async-done(((f32[1024,128]{1,0:T(8,128)}), f32[1024,128]{1,0:T(8,128)}) %all-reduce.3.cloned.1.call-update) | async-done | bytes 524304 | tf_op jit(solution)/shard_map/psum | solution.py:55
  374.3 1.2 collective-permute-start
  375.5 13.6 %collective-permute-done = f32[1024,128]{1,0:T(8,128)S(1)} collective-permute-done((f32[1024,128]{1,0:T(8,128)}, f32[1024,128]{1,0:T(8,128)S(1)}, u32[]{:S(2)}, u32[]{:S(2)}) %collective-permute-start) | collective-permute-done | bytes 524320 | tf_op jit(solution)/shard_map/ppermute | solution.py:58
  389.1 13.7 %collective-permute-done.1 = f32[1024,128]{1,0:T(8,128)S(1)} collective-permute-done((f32[1024,128]{1,0:T(8,128)S(1)}, f32[1024,128]{1,0:T(8,128)S(1)}, u32[]{:S(2)}, u32[]{:S(2)}) %collective-permute-start.1) | collective-permute-done | bytes 524320 | tf_op jit(solution)/shard_map/ppermute | solution.py:58
  402.7 0.2 collective-permute-start.2
  402.9 12.8 %collective-permute-done.2 = f32[1024,128]{1,0:T(8,128)} collective-permute-done((f32[1024,128]{1,0:T(8,128)S(1)}, f32[1024,128]{1,0:T(8,128)}, u32[]{:S(2)}, u32[]{:S(2)}) %collective-permute-start.2) | collective-permute-done | bytes 524320 | tf_op jit(solution)/shard_map/ppermute | solution.py:58
  415.7 4.9 fusion.10
  420.7 1.3 copy-done.4
  422.0 3.5 fusion.36
  425.5 0.1 copy.14
  425.6 11.7 %cholesky.44 = f32[128,128]{1,0:T(8,128)S(1)} custom-call(f32[128,128]{1,0:T(8,128)S(1)} %fusion.29), custom_call_target="Cholesky" | custom-call | tf_op jit(solution)/shard_map/jit(cholesky)/cholesky | solution.py:70
  437.4 0.6 compare_reduce_fusion.1
  438.0 0.7 fusion.24
  438.7 10.0 %custom-call.6 = f32[1,128,128]{1,2,0:T(8,128)S(1)} custom-call(f32[1,128,128]{2,1,0:T(8,128)S(1)} %fusion.24), custom_call_target="InvertDiagBlocksLowerTriangular" | custom-call | tf_op jit(solution)/shard_map/jit(_solve_triangular)/triangular_solve | solution.py:71
  448.7 3.7 fusion.16
  452.4 7.6 %fusion.20 = f32[1024,128]{1,0:T(8,128)} fusion(f32[1024,1024]{1,0:T(8,128)S(1)} %copy-done.2, f32[128,4096]{1,0:T(8,128)S(1)} %fusion.16, s32[]{:T(128)S(6)} %select_n.20), kind=kOutput, calls=%fused_computation.38 | convolution fusion | flops 1610612736 | bytes 5242884 | tf_op jit(solution)/shard_map/dot_general | solution.py:48
  460.0 39.1 %all-reduce.5.cloned.1.call-done = f32[1024,128]{1,0:T(8,128)} async-done(((f32[1024,128]{1,0:T(8,128)}), f32[1024,128]{1,0:T(8,128)}) %all-reduce.5.cloned.1.call-update) | async-done | bytes 524304 | tf_op jit(solution)/shard_map/psum | solution.py:55
  499.1 1.2 collective-permute-start.3
  500.3 13.6 %collective-permute-done.3 = f32[1024,128]{1,0:T(8,128)S(1)} collective-permute-done((f32[1024,128]{1,0:T(8,128)}, f32[1024,128]{1,0:T(8,128)S(1)}, u32[]{:S(2)}, u32[]{:S(2)}) %collective-permute-start.3) | collective-permute-done | bytes 524320 | tf_op jit(solution)/shard_map/ppermute | solution.py:58
  513.9 13.7 %collective-permute-done.4 = f32[1024,128]{1,0:T(8,128)S(1)} collective-permute-done((f32[1024,128]{1,0:T(8,128)S(1)}, f32[1024,128]{1,0:T(8,128)S(1)}, u32[]{:S(2)}, u32[]{:S(2)}) %collective-permute-start.4) | collective-permute-done | bytes 524320 | tf_op jit(solution)/shard_map/ppermute | solution.py:58
  527.5 0.4 collective-permute-start.5
  527.9 12.8 %collective-permute-done.5 = f32[1024,128]{1,0:T(8,128)} collective-permute-done((f32[1024,128]{1,0:T(8,128)S(1)}, f32[1024,128]{1,0:T(8,128)}, u32[]{:S(2)}, u32[]{:S(2)}) %collective-permute-start.5) | collective-permute-done | bytes 524320 | tf_op jit(solution)/shard_map/ppermute | solution.py:58
  540.8 4.9 fusion.3
  545.7 1.3 copy-done.3
  547.1 3.5 fusion.37
  550.6 0.1 copy.15
  550.7 11.7 %cholesky.55 = f32[128,128]{1,0:T(8,128)S(1)} custom-call(f32[128,128]{1,0:T(8,128)S(1)} %fusion.27), custom_call_target="Cholesky" | custom-call | tf_op jit(solution)/shard_map/jit(cholesky)/cholesky | solution.py:70
  562.5 0.6 compare_reduce_fusion
  563.1 0.7 fusion.25
  563.8 9.9 %custom-call.7 = f32[1,128,128]{1,2,0:T(8,128)S(1)} custom-call(f32[1,128,128]{2,1,0:T(8,128)S(1)} %fusion.25), custom_call_target="InvertDiagBlocksLowerTriangular" | custom-call | tf_op jit(solution)/shard_map/jit(_solve_triangular)/triangular_solve | solution.py:71
  573.7 3.5 fusion.14
  577.3 0.8 copy.16
  (22 shorter events, 0.3 us)
Async XLA Ops:
  7.2 16.9 %copy-start = (bf16[8,1024,128]{2,1,0:T(8,128)(2,1)S(1)}, bf16[8,1024,128]{2,1,0:T(8,128)(2,1)}, u32[]{:S(2)}) copy-start(bf16[8,1024,128]{2,1,0:T(8,128)(2,1)} %param.11) | copy-start | bytes 6291460
  7.2 16.9 %copy-start.5 = (bf16[1024,8,16]{0,2,1:T(8,128)(2,1)S(1)}, bf16[1024,8,16]{0,2,1:T(8,128)(2,1)}, u32[]{:S(2)}) copy-start(bf16[1024,8,16]{0,2,1:T(8,128)(2,1)} %param.9) | copy-start | bytes 786436
  7.2 46.2 %all-gather.3.cloned.1.call-start = ((), (), s32[]{:S(2)}) async-start(), calls=%async_computation.1 | async-start | bytes 1310720 | tf_op jit(solution)/shard_map/all_gather | solution.py:25
  25.6 222.5 %reduce-scatter.2.cloned.1.call-start = ((), (), s32[]{:S(2)}) async-start(), calls=%async_computation.2 | async-start | bytes 17301504 | tf_op jit(solution)/shard_map/reduce_scatter | solution.py:35
  62.8 261.8 %all-gather.5.cloned.1.call-start = ((), (), s32[]{:S(2)}) async-start(), calls=%async_computation.3 | async-start | bytes 4718592 | tf_op jit(solution)/shard_map/all_gather | solution.py:43
  248.1 126.2 %all-reduce.3.cloned.1.call-start = ((), (), s32[]{:S(2)}) async-start(), calls=%async_computation.4 | async-start | bytes 1048576 | tf_op jit(solution)/shard_map/psum | solution.py:55
  327.2 2.0 copy-start.1
  337.8 161.3 %all-reduce.5.cloned.1.call-start = ((), (), s32[]{:S(2)}) async-start(), calls=%async_computation.5 | async-start | bytes 1048576 | tf_op jit(solution)/shard_map/psum | solution.py:55
  374.3 14.8 %collective-permute-start = (f32[1024,128]{1,0:T(8,128)}, f32[1024,128]{1,0:T(8,128)S(1)}, u32[]{:S(2)}, u32[]{:S(2)}) collective-permute-start(f32[1024,128]{1,0:T(8,128)} %all-reduce.3.cloned.1.call-done), channel_id=1, source_target_pairs={{0,4},{4,8},{8,12},{12,0},{1,5},{5,9},{9,13},{13,1},{2,6},{6,10},{... | collective-permute-start | bytes 1572872 | tf_op jit(solution)/shard_map/ppermute | solution.py:58
  389.0 13.7 %collective-permute-start.1 = (f32[1024,128]{1,0:T(8,128)S(1)}, f32[1024,128]{1,0:T(8,128)S(1)}, u32[]{:S(2)}, u32[]{:S(2)}) collective-permute-start(f32[1024,128]{1,0:T(8,128)S(1)} %collective-permute-done), channel_id=1, source_target_pairs={{0,4},{4,8},{8,12},{12,0},{1,5},{5,9},{9,13},{13,1},{2,6},{6,10},{... | collective-permute-start | bytes 1572872 | tf_op jit(solution)/shard_map/ppermute | solution.py:58
  402.7 13.0 %collective-permute-start.2 = (f32[1024,128]{1,0:T(8,128)S(1)}, f32[1024,128]{1,0:T(8,128)}, u32[]{:S(2)}, u32[]{:S(2)}) collective-permute-start(f32[1024,128]{1,0:T(8,128)S(1)} %collective-permute-done.1), channel_id=1, source_target_pairs={{0,4},{4,8},{8,12},{12,0},{1,5},{5,9},{9,13},{13,1},{2,6},{6,10},{... | collective-permute-start | bytes 1572872 | tf_op jit(solution)/shard_map/ppermute | solution.py:58
  420.6 1.3 copy-start.4
  448.7 3.7 copy-start.2
  499.1 14.8 %collective-permute-start.3 = (f32[1024,128]{1,0:T(8,128)}, f32[1024,128]{1,0:T(8,128)S(1)}, u32[]{:S(2)}, u32[]{:S(2)}) collective-permute-start(f32[1024,128]{1,0:T(8,128)} %all-reduce.5.cloned.1.call-done), channel_id=1, source_target_pairs={{0,4},{4,8},{8,12},{12,0},{1,5},{5,9},{9,13},{13,1},{2,6},{6,10},{... | collective-permute-start | bytes 1572872 | tf_op jit(solution)/shard_map/ppermute | solution.py:58
  513.9 13.7 %collective-permute-start.4 = (f32[1024,128]{1,0:T(8,128)S(1)}, f32[1024,128]{1,0:T(8,128)S(1)}, u32[]{:S(2)}, u32[]{:S(2)}) collective-permute-start(f32[1024,128]{1,0:T(8,128)S(1)} %collective-permute-done.3), channel_id=1, source_target_pairs={{0,4},{4,8},{8,12},{12,0},{1,5},{5,9},{9,13},{13,1},{2,6},{6,10},{... | collective-permute-start | bytes 1572872 | tf_op jit(solution)/shard_map/ppermute | solution.py:58
  527.5 13.2 %collective-permute-start.5 = (f32[1024,128]{1,0:T(8,128)S(1)}, f32[1024,128]{1,0:T(8,128)}, u32[]{:S(2)}, u32[]{:S(2)}) collective-permute-start(f32[1024,128]{1,0:T(8,128)S(1)} %collective-permute-done.4), channel_id=1, source_target_pairs={{0,4},{4,8},{8,12},{12,0},{1,5},{5,9},{9,13},{13,1},{2,6},{6,10},{... | collective-permute-start | bytes 1572872 | tf_op jit(solution)/shard_map/ppermute | solution.py:58
  545.7 1.3 copy-start.3
Sparse Core Ops, SparseCore 0:
  25.7 27.5 all-gather.2
  62.9 185.1 reduce-scatter.1
  250.4 74.1 all-gather.4
  337.9 36.3 all-reduce.2
  460.1 38.9 all-reduce.4
